TPU v7x, 32 devices: a whole 2x2x4 slice. The times are simulated.
32 devices in a mesh: slab: 8 (over y, x, core), chan: 4 (over z).
Axes of the slice: x: 2, y: 2, z: 4, core: 2. Of those that a mesh axis runs over, the one named last changes fastest.
Arguments:
- field: bfloat16 [1, 128, 128, 128, 128], P(None, 'chan', 'slab'), may hold values from -6 to 6
- local_weight: bfloat16 [128, 128], replicated, may hold values from -0.5 to 0.5
- bias: float32 [128], replicated, may hold values from -3 to 3
- spec_weight: float32 [2, 128, 128, 4096], P(None, 'chan', None, 'slab'), may hold values from -4.2 to 4.2
Outputs:
- activated: bfloat16 [1, 128, 128, 128, 128], P(None, 'chan', 'slab')
All inputs are finite; a program needn't handle non-finite values.
Results may differ from a plain program's by a relative error of at most 0.0026.
Values may be sent and summed in bfloat16 or wider, within the bound.
A program may use at most 384 MiB of HBM per device.

v0:
```python
import math

import jax
import jax.numpy as jnp
from jax import lax
from jax.sharding import PartitionSpec as P

GRID = 128
KEEP = 16
MODES = 4096


PRECISE = lax.Precision.HIGHEST


def mode_freqs(count, length):
    index = jnp.arange(count, dtype=jnp.int32)
    return jnp.where(index < count // 2, index, index + (length - count))


def phase_table(freqs, positions, length):
    product_int = freqs[:, None] * positions[None, :] % length
    return 2.0 * math.pi * product_int.astype(jnp.float32) / length


def build_tables(zcells):
    xfreq = mode_freqs(KEEP, GRID)
    zfreq = jnp.arange(KEEP, dtype=jnp.int32)
    cells = jnp.arange(GRID, dtype=jnp.int32)
    angle_x = phase_table(xfreq, cells, GRID)
    angle_z = phase_table(zfreq, zcells, GRID)
    cos_x, sin_x = (jnp.cos(angle_x), jnp.sin(angle_x))
    cos_z, sin_z = (jnp.cos(angle_z), jnp.sin(angle_z))
    table_x = jnp.concatenate([cos_x, -sin_x], 0).astype(jnp.bfloat16)
    fold_factor = jnp.where(zfreq == 0, 1.0, 2.0).astype(jnp.float32)
    return (cos_x, sin_x, cos_z, sin_z, table_x, fold_factor)


def product(form, left, right):
    return jnp.einsum(form, left, right, precision=PRECISE)


def on_device(field, local_weight, bias, spec_weight):
    samples, chan_local, zdepth = (field.shape[0], field.shape[1], field.shape[2])
    zcells = lax.axis_index("slab") * zdepth + jnp.arange(zdepth, dtype=jnp.int32)
    cos_x, sin_x, cos_z, sin_z, table_x, fold_factor = build_tables(zcells)
    section_x = jnp.einsum("kx,bczxy->bczky", table_x, field, preferred_element_type=jnp.float32)
    part_real = section_x[:, :, :, :KEEP]
    part_imag = section_x[:, :, :, KEEP:]
    wave_real = product("bczky,jy->bczkj", part_real, cos_x) + product(
        "bczky,jy->bczkj", part_imag, sin_x
    )
    wave_imag = product("bczky,jy->bczkj", part_imag, cos_x) - product(
        "bczky,jy->bczkj", part_real, sin_x
    )
    four_real = product("bczkj,lz->bckjl", wave_real, cos_z) + product(
        "bczkj,lz->bckjl", wave_imag, sin_z
    )
    four_imag = product("bczkj,lz->bckjl", wave_imag, cos_z) - product(
        "bczkj,lz->bckjl", wave_real, sin_z
    )
    partial_value = jnp.stack(
        [
            four_real.reshape(samples, chan_local, MODES),
            four_imag.reshape(samples, chan_local, MODES),
        ],
        1,
    )
    owned = lax.psum_scatter(partial_value, "slab", scatter_dimension=3, tiled=True)
    piece = lax.all_gather(owned, "chan", axis=2, tiled=True)
    weight_real = spec_weight[0]
    weight_imag = spec_weight[1]
    coef_real = piece[:, 0]
    coef_imag = piece[:, 1]
    mixed_real = product("bcm,ocm->bom", coef_real, weight_real) - product(
        "bcm,ocm->bom", coef_imag, weight_imag
    )
    mixed_imag = product("bcm,ocm->bom", coef_real, weight_imag) + product(
        "bcm,ocm->bom", coef_imag, weight_real
    )
    mixed = jnp.stack([mixed_real, mixed_imag], 1)
    spectrum = lax.all_gather(mixed, "slab", axis=3, tiled=True)
    spectral = spectrum.reshape(samples, 2, chan_local, KEEP, KEEP, KEEP) * fold_factor
    spectral_real, spectral_imag = (spectral[:, 0], spectral[:, 1])
    plane_real = product("bokjl,lz->bozkj", spectral_real, cos_z) - product(
        "bokjl,lz->bozkj", spectral_imag, sin_z
    )
    plane_imag = product("bokjl,lz->bozkj", spectral_imag, cos_z) + product(
        "bokjl,lz->bozkj", spectral_real, sin_z
    )
    line_real = product("bozkj,kx->bozxj", plane_real, cos_x) - product(
        "bozkj,kx->bozxj", plane_imag, sin_x
    )
    line_imag = product("bozkj,kx->bozxj", plane_imag, cos_x) + product(
        "bozkj,kx->bozxj", plane_real, sin_x
    )
    mapped = jnp.einsum(
        "oc,bczxy->bozxy",
        local_weight,
        lax.all_to_all(field, "chan", split_axis=3, concat_axis=1, tiled=True),
        preferred_element_type=jnp.float32,
    )
    local = lax.all_to_all(mapped, "chan", split_axis=1, concat_axis=3, tiled=True)
    inverse = (
        product("bozxj,jy->bozxy", line_real, cos_x) - product("bozxj,jy->bozxy", line_imag, sin_x)
    ) / GRID**3
    offset = lax.dynamic_slice_in_dim(bias, lax.axis_index("chan") * chan_local, chan_local, 0)
    total = inverse + local + offset[None, :, None, None, None]
    return jax.nn.gelu(total, approximate=False).astype(jnp.bfloat16)


def solution(mesh):
    placed = (P(None, "chan", "slab", None, None), P(), P(), P(None, "chan", None, "slab"))
    return jax.shard_map(
        on_device,
        mesh=mesh,
        in_specs=placed,
        out_specs=P(None, "chan", "slab", None, None),
        check_vma=False,
    )
```

profile of v0, /device:TPU:0, one launch (start us, length us, event | category | flops | bytes accessed | tf_op | source)
XLA Modules:
  0.0 1561.9 jit_solution(10960533788971022763)
XLA Ops:
  6.5 11.1 copy.121
  17.6 368.9 %all_to_all.33 = bf16[1,32,16,128,128]{4,2,1,0,3:T(8,128)(2,1)S(1)} all-to-all(bf16[1,32,16,128,128]{4,2,1,0,3:T(8,128)(2,1)S(1)} %copy.121), channel_id=1, replica_groups=mesh['slab'=8,'chan'=4] {'chan'}, dimensions={3} | all-to-all | bytes 33554432 | tf_op jit(solution)/shard_map/all_to_all | solution.py:100
  386.5 36.5 %copy.122 = bf16[1,32,16,128,128]{4,3,2,1,0:T(8,128)(2,1)S(1)} copy(bf16[1,32,16,128,128]{4,2,1,0,3:T(8,128)(2,1)S(1)} %all_to_all.33) | data formatting | bytes 33554432 | tf_op jit(solution)/shard_map/all_to_all | solution.py:100
  423.1 9.0 copy.123
  432.1 44.2 %fusion.15 = f32[1,128,16,32,128]{1,4,3,2,0:T(8,128)} fusion(bf16[128,16,32,128]{3,2,1,0:T(8,128)(2,1)} %bitcast.199, bf16[128,128]{1,0:T(8,128)(2,1)S(1)} %copy-done), kind=kOutput, calls=%fused_computation.26 | convolution fusion | flops 2147483648 | bytes 50364416 | tf_op jit(solution)/shard_map/oc,bczxy->bozxy/dot_general | solution.py:97
  476.4 34.6 %copy.125 = f32[1,128,16,32,128]{4,3,2,0,1:T(8,128)} copy(f32[1,128,16,32,128]{1,4,3,2,0:T(8,128)} %fusion.15) | data formatting | bytes 67108864 | tf_op jit(solution)/shard_map/oc,bczxy->bozxy/transpose | solution.py:97
  511.0 9.7 all-to-all-start.1
  520.9 7.0 fusion.29
  531.5 5.3 fusion.32
  536.8 4.0 copy.104
  540.9 5.8 fusion.25
  546.6 5.2 fusion.33
  551.9 5.2 copy.106
  559.1 5.0 convolution_add_fusion
  576.1 104.8 %copy.165 = f32[1,2,32,4096]{1,0,2,3:T(1,128)} copy(f32[1,2,32,4096]{3,1,0,2:T(2,128)S(1)} %pad_maximum_fusion) | data formatting | bytes 2097152
  680.9 203.2 %bitcast_reduce_fusion = f32[4096,32,2]{2,1,0:T(8,128)} fusion(f32[1,2,32,4096]{1,0,2,3:T(1,128)} %copy.165), kind=kLoop, calls=%fused_computation | loop fusion | bytes 2097152
  884.1 54.9 %reshape.236 = f32[4096,64]{1,0:T(8,128)} reshape(f32[4096,32,2]{2,1,0:T(8,128)} %bitcast_reduce_fusion) | data formatting | bytes 2097152
  939.1 42.7 %reduce-scatter.4.cloned.1.call-done = f32[512,64]{1,0:T(8,128)} async-done(((f32[4096,64]{1,0:T(8,128)}), f32[512,64]{1,0:T(8,128)}) %reduce-scatter.4.cloned.1.call-update) | async-done | bytes 131088
  981.8 15.6 reshape.237
  997.4 16.2 %copy.166 = f32[1,2,32,512]{3,1,0,2:T(2,128)S(1)} copy(f32[1,2,32,512]{1,0,2,3:T(1,128)} %bitcast.202) | data formatting | bytes 262144
  1013.6 238.9 %all_gather.6 = f32[1,2,128,512]{3,1,0,2:T(2,128)S(1)} all-gather(f32[1,2,32,512]{3,1,0,2:T(2,128)S(1)} %copy.166), channel_id=1, replica_groups=mesh['slab'=8,'chan'=4] {'chan'}, dimensions={2}, use_global_device_ids=true | all-gather | bytes 655360 | tf_op jit(solution)/shard_map/all_gather | solution.py:70
  1252.9 8.1 fusion.18
  1261.9 24.5 %all-gather.2.cloned.1.call-done = f32[1,2,32,4096]{3,2,1,0:T(8,128)} async-done(((f32[1,2,32,512]{3,2,1,0:T(8,128)}), f32[1,2,32,4096]{3,2,1,0:T(8,128)}) %all-gather.2.cloned.1.call-update) | async-done | bytes 1048592 | tf_op jit(solution)/shard_map/all_gather | solution.py:82
  1286.4 4.0 copy.114
  1299.4 7.3 fusion.38
  1308.8 7.1 fusion.42
  1316.0 8.7 add_bitcast_fusion
  1324.7 7.3 subtract_bitcast_fusion
  1332.0 56.7 %fusion.23 = f32[32,16,128,128]{3,2,1,0:T(8,128)} fusion(f32[32,16,128,16]{2,0,3,1:T(8,128)S(1)} %subtract_bitcast_fusion, s32[16]{0:T(128)S(1)} %compare_select_fusion), kind=kOutput, calls=%fused_computation.38 | convolution fusion | flops 1610641408 | bytes 37748800 | tf_op jit(solution)/shard_map/bozxj,jy->bozxy/dot_general | solution.py:40
  1388.7 27.3 %copy.126 = f32[1,32,16,4,32,128]{5,4,3,2,1,0:T(8,128)} copy(f32[1,32,16,4,32,128]{5,4,2,1,3,0:T(8,128)} %bitcast.75) | data formatting | bytes 67108864 | tf_op jit(solution)/shard_map/all_to_all | solution.py:103
  1416.0 4.4 copy-done.4
  1421.6 133.3 %fusion.14 = bf16[1,32,16,128,128]{4,3,2,1,0:T(8,128)(2,1)} fusion(f32[32]{0:T(128)S(1)} %dynamic_slice.3, f32[32,16,128,128]{3,2,1,0:T(8,128)} %bitcast.201, f32[32,16,128,128]{3,2,1,0:T(8,128)S(1)} %copy-done.4, f32[32,16,128,16]{2,0,3,1:T(8,128)S(1)} %copy-done.5, s32[16]{0:T(128)S(1)} %compare_select_fusion), kind=kOutput, calls=%fused_computation.25 | convolution fusion | flops 2189455360 | bytes 88080576 | tf_op jit(solution)/shard_map/bozxj,jy->bozxy/dot_general | solution.py:40
  (40 shorter events, 31.2 us)
Async XLA Ops:
  6.5 425.6 %copy-start = (bf16[128,128]{1,0:T(8,128)(2,1)S(1)}, bf16[128,128]{1,0:T(8,128)(2,1)}, u32[]{:S(2)}) copy-start(bf16[128,128]{1,0:T(8,128)(2,1)} %param.5) | copy-start | bytes 98308
  511.0 877.7 %all-to-all-start.1 = ((f32[1,128,16,32,128]{4,3,2,0,1:T(8,128)}), f32[1,128,16,32,128]{4,3,2,0,1:T(8,128)}, u32[]{:S(2)}, u32[]{:S(2)}) async-start(f32[1,128,16,32,128]{4,3,2,0,1:T(8,128)} %copy.125), calls=%async_computation.1 | async-start | bytes 67108864 | tf_op jit(solution)/shard_map/all_to_all | solution.py:103
  520.7 461.1 %reduce-scatter.4.cloned.1.call-start = ((), (), s32[]{:S(2)}) async-start(), calls=%async_computation.4 | async-start | bytes 2359296
  527.9 3.6 copy-start.2
  540.9 5.8 copy-start.3
  939.0 347.4 %all-gather.2.cloned.1.call-start = ((), (), s32[]{:S(2)}) async-start(), calls=%async_computation.3 | async-start | bytes 1179648 | tf_op jit(solution)/shard_map/all_gather | solution.py:82
  1252.9 8.9 copy-start.6
  1388.7 31.8 %copy-start.4 = (f32[32,16,128,128]{3,2,1,0:T(8,128)S(1)}, f32[32,16,128,128]{3,2,1,0:T(8,128)}, u32[]{:S(2)}) copy-start(f32[32,16,128,128]{3,2,1,0:T(8,128)} %fusion.23) | copy-start | bytes 100663296
  1388.7 33.0 %copy-start.5 = (f32[32,16,128,16]{2,0,3,1:T(8,128)S(1)}, f32[32,16,128,16]{2,0,3,1:T(8,128)}, u32[]{:S(2)}) copy-start(f32[32,16,128,16]{2,0,3,1:T(8,128)} %add_bitcast_fusion) | copy-start | bytes 12582916
  1421.6 133.3 %copy-start.1 = (bf16[128,128]{1,0:T(8,128)(2,1)S(1)}, bf16[128,128]{1,0:T(8,128)(2,1)}, u32[]{:S(2)}) copy-start(bf16[128,128]{1,0:T(8,128)(2,1)} %param.5) | copy-start | bytes 98308
Sparse Core Ops, SparseCore 0:
  939.2 42.5 reduce-scatter.3
  1261.9 24.4 all-gather.1
where the time goes:
time: 1570 us; the launch traced here: 1560 us
  blocking collectives  608 us (39%)
  local copies, waits for them, and re-layouts  537 us (34%)
  matrix products  314 us (20%)
  waiting for transfers between devices  67.3 us (4%)
    unnamed x21, local copies, waits for them, and re-layouts  411 us
    all_to_all x1, blocking collectives, on_device(): lax.all_to_all(field, 'chan', split_axis=3, concat_axis=1, tiled=True)  369 us
    dot_general x18, matrix products, product(): return jnp.einsum(form, left, right, precision=PRECISE)  262 us
    all_gather x1, blocking collectives, on_device(): piece = lax.all_gather(owned, 'chan', axis=2, tiled=True)  239 us
    all_to_all x2, local copies, waits for them, and re-layouts, on_device(): lax.all_to_all(field, 'chan', split_axis=3, concat_axis=1, tiled=True)  45.6 us
    dot_general x1, matrix products, on_device(): jnp.einsum('oc,bczxy->bozxy', local_weight, lax.all_to_all(field, 'chan',...  44.2 us
    unnamed x3, waiting for transfers between devices  42.7 us
    transpose x1, local copies, waits for them, and re-layouts, on_device(): jnp.einsum('oc,bczxy->bozxy', local_weight, lax.all_to_all(field, 'chan',...  34.6 us
  transfers between devices with their start and end apart: 3, of which 2 were waited for; matrix products, arithmetic and copies ran while one was open for 36% of the time, Pallas kernels for 0%

commit v1 on v0

v1 whole, which is shorter than its diff:
```python
import math

import jax
import jax.numpy as jnp
from jax import lax
from jax.experimental import pallas as pl
from jax.experimental.pallas import tpu as pltpu
from jax.sharding import PartitionSpec as P

KEEP = 16
ROWS = 16
CHUNKS = (2, 2, 2, 2, 2, 2, 2, 1, 1)
WIDE_CHUNKS = 4

PRECISE = lax.Precision.HIGHEST


def mode_freqs(count, length):
    index = jnp.arange(count, dtype=jnp.int32)
    return jnp.where(index < count // 2, index, index + (length - count))


def phase_table(freqs, positions, length):
    product_int = freqs[:, None] * positions[None, :] % length
    return 2.0 * math.pi * product_int.astype(jnp.float32) / length


def product(form, left, right):
    return jnp.einsum(form, left, right, precision=PRECISE)


def map_kernel(kron_ref, own_ref, a_ref, b_ref, c_ref, mine_ref, part_ref):
    chans, _, xcells, ycells = own_ref.shape
    depth = chans * ROWS
    pair = 2 * ROWS

    @pl.loop(0, xcells // pair)
    def _(step):
        base = pl.multiple_of(step * pair, pair)
        total = None
        for index, ref in enumerate((own_ref, a_ref, b_ref, c_ref)):
            left = ref[:, 0, pl.ds(base, ROWS), :].reshape(depth, ycells)
            right = ref[:, 0, pl.ds(base + ROWS, ROWS), :].reshape(depth, ycells)
            block = jnp.concatenate([left, right], 1)
            term = jnp.dot(
                kron_ref[:, index * depth : (index + 1) * depth],
                block,
                preferred_element_type=jnp.float32,
            )
            total = term if total is None else total + term
        for half in range(2):
            piece = total[:, half * ycells : (half + 1) * ycells]
            piece = piece.reshape(2 * chans, ROWS, ycells)
            rows = pl.ds(base + half * ROWS, ROWS)
            mine_ref[:, 0, rows, :] = piece[:chans]
            part_ref[:, 0, rows, :] = piece[chans:].astype(part_ref.dtype)


def map_chunk(kron, field, others, start, depth, part_type):
    chans, _, xcells, ycells = field.shape
    block = (chans, 1, xcells, ycells)
    small = pl.BlockSpec(block, lambda z: (0, z, 0, 0))
    shape = (chans, depth, xcells, ycells)
    cost = 2 * 2 * kron.shape[0] * kron.shape[1] // 2 * depth * xcells * ycells // ROWS
    return pl.pallas_call(
        map_kernel,
        grid=(depth,),
        in_specs=[
            pl.BlockSpec(kron.shape, lambda z: (0, 0)),
            pl.BlockSpec(block, lambda z: (0, z + start, 0, 0)),
            small,
            small,
            small,
        ],
        out_specs=[small, small],
        out_shape=[
            jax.ShapeDtypeStruct(shape, jnp.float32),
            jax.ShapeDtypeStruct(shape, part_type),
        ],
        compiler_params=pltpu.CompilerParams(vmem_limit_bytes=44 * 2**20),
        cost_estimate=pl.CostEstimate(
            flops=cost, bytes_accessed=16 * chans * depth * xcells * ycells, transcendentals=0
        ),
        name="map_chunk",
    )(kron, field, *others)


def finish_kernel(table_ref, bias_ref, wave_ref, mine_ref, recv_ref, *rest):
    out_ref = rest[-1]
    table = table_ref[...]

    @pl.loop(0, out_ref.shape[0])
    def _(o):
        inverse = jnp.dot(table, wave_ref[o, 0], preferred_element_type=jnp.float32)
        total = inverse + (mine_ref[o, 0] + recv_ref[o, 0].astype(jnp.float32)) + bias_ref[o]
        value = 0.5 * total * (1.0 + lax.erf(total * (0.5**0.5)))
        out_ref[o, 0] = value.astype(out_ref.dtype)


def finish_chunk(table, bias, wave, mine, recv, out, start, whole_depth):
    chans, depth, xcells, ycells = mine.shape
    part = min(16, chans)
    block = (part, 1, xcells, ycells)
    small = pl.BlockSpec(block, lambda c, z: (c, z, 0, 0))
    placed = pl.BlockSpec(block, lambda c, z: (c, z + start, 0, 0))
    operands = [table, bias, wave, mine, recv]
    specs = [
        pl.BlockSpec(table.shape, lambda c, z: (0, 0)),
        pl.BlockSpec((part, 1, ycells), lambda c, z: (c, 0, 0)),
        pl.BlockSpec((part, 1, wave.shape[2], ycells), lambda c, z: (c, z + start, 0, 0)),
        small,
        small,
    ]
    aliases = {}
    if out is not None:
        aliases = {len(operands): 0}
        operands.append(out)
        specs.append(pl.BlockSpec(memory_space=pl.ANY))
    count = chans * depth * xcells * ycells
    return pl.pallas_call(
        finish_kernel,
        grid=(chans // part, depth),
        in_specs=specs,
        out_specs=placed,
        out_shape=jax.ShapeDtypeStruct((chans, whole_depth, xcells, ycells), jnp.bfloat16),
        input_output_aliases=aliases,
        compiler_params=pltpu.CompilerParams(vmem_limit_bytes=40 * 2**20),
        cost_estimate=pl.CostEstimate(
            flops=count * 60, bytes_accessed=count * 12, transcendentals=count
        ),
        name="finish_chunk",
    )(*operands)


def forward_modes(field, table_x, cos_yz, sin_yz):
    chans, zdepth, xcells, ycells = field.shape
    section = jnp.einsum("kx,czxy->ckzy", table_x, field, preferred_element_type=jnp.float32)
    section = section.reshape(chans * 2 * KEEP, zdepth * ycells)
    both = jnp.concatenate([cos_yz, -sin_yz], 1)
    four = jnp.dot(section, both, precision=PRECISE)
    four = four.reshape(chans, 2 * KEEP, 2, KEEP * KEEP)
    real = four[:, :KEEP, 0] - four[:, KEEP:, 1]
    imag = four[:, KEEP:, 0] + four[:, :KEEP, 1]
    return jnp.stack([real, imag], 0).transpose(2, 0, 1, 3)


def gather_line(value, axis, size):
    here = lax.axis_index(axis)
    pieces = jnp.zeros((size,) + value.shape, value.dtype)
    pieces = lax.dynamic_update_index_in_dim(pieces, value, here, 0)
    for shift in range(1, size):
        moved = lax.ppermute(value, axis, [(i, (i + shift) % size) for i in range(size)])
        pieces = lax.dynamic_update_index_in_dim(pieces, moved, (here + size - shift) % size, 0)
    return pieces


def mix(piece, spec_weight):
    chans = piece.shape[0] * piece.shape[3]
    coef = piece.transpose(2, 0, 3, 1, 4).reshape(2, chans, -1)
    weight_real, weight_imag = spec_weight[0], spec_weight[1]
    real = product("cm,ocm->om", coef[0], weight_real) - product("cm,ocm->om", coef[1], weight_imag)
    imag = product("cm,ocm->om", coef[0], weight_imag) + product("cm,ocm->om", coef[1], weight_real)
    return jnp.stack([real, imag], 0)


def on_device(slabs, lines, field, local_weight, bias, spec_weight):
    _, chans, zdepth, xcells, ycells = field.shape
    field = field[0]
    here = lax.axis_index("chan")
    zcells = lax.axis_index("slab") * zdepth + jnp.arange(zdepth, dtype=jnp.int32)
    freqs = mode_freqs(KEEP, xcells)
    zfreq = jnp.arange(KEEP, dtype=jnp.int32)
    angle_x = phase_table(freqs, jnp.arange(xcells, dtype=jnp.int32), xcells)
    angle_z = phase_table(zfreq, zcells, zdepth * slabs)
    cos_x, sin_x = jnp.cos(angle_x), jnp.sin(angle_x)
    cos_z, sin_z = jnp.cos(angle_z), jnp.sin(angle_z)
    table_x = jnp.concatenate([cos_x, -sin_x], 0).astype(jnp.bfloat16)
    fold = jnp.where(zfreq == 0, 1.0, 2.0).astype(jnp.float32)

    def joined(form, shape):
        def outer(z_part, y_part):
            return jnp.einsum(form, z_part, y_part, precision=PRECISE)

        cosine = outer(cos_z, cos_x) - outer(sin_z, sin_x)
        sine = outer(sin_z, cos_x) + outer(cos_z, sin_x)
        return cosine.reshape(shape), sine.reshape(shape)

    modes = KEEP * KEEP

    def local_parts():
        offset = lax.dynamic_slice_in_dim(bias, here * chans, chans, 0)
        return jnp.broadcast_to(offset[:, None, None], (chans, 1, ycells))

    bias_rows = local_parts()

    hubs = lines == 4
    if hubs:
        last = lines - 1
        partner = here + 1 - 2 * (here % 2)
        order = [here, last - here, partner, last - partner]

        def weight_block(out_block, in_block):
            return lax.dynamic_slice(
                local_weight, (out_block * chans, in_block * chans), (chans, chans)
            )

        top = jnp.concatenate([weight_block(here, block) for block in order], 1)
        low = [weight_block(partner, block) for block in order]
        low[2] = jnp.zeros_like(low[2])
        pair_weight = jnp.concatenate([top, jnp.concatenate(low, 1)], 0)
        eye = jnp.eye(ROWS, dtype=pair_weight.dtype)
        kron = (pair_weight[:, None, :, None] * eye[None, :, None, :]).reshape(
            2 * chans * ROWS, lines * chans * ROWS
        )
        swap = [(1, 2), (2, 1)]
        near = [(0, 1), (3, 2)]
        far = [(0, 2), (3, 1)]
        back = [(1, 0), (2, 3)]
        unit = zdepth // sum(CHUNKS)
        depths = [unit * depth for depth in CHUNKS]
        starts = [sum(depths[:i]) for i in range(len(depths))]
        arrived, parts = [], []
        for index, (start, depth) in enumerate(zip(starts, depths)):
            send = lax.slice_in_dim(field, start, start + depth, axis=1)
            if index >= 2:
                send, arrived[index - 2] = lax.optimization_barrier((send, arrived[index - 2]))
            arrived.append([lax.ppermute(send, "chan", pairs) for pairs in (swap, far, near)])
        for index, (start, depth) in enumerate(zip(starts, depths)):
            swapped, from_far, from_near = arrived[index]
            kind = jnp.float32 if index < WIDE_CHUNKS else jnp.bfloat16
            mine, part = map_chunk(
                kron, field, (swapped, from_near, from_far), start, depth, kind
            )
            parts.append((mine, lax.ppermute(part, "chan", back)))

    cos_yz, sin_yz = joined("lz,ky->zykl", (zdepth * ycells, modes))
    partial_value = forward_modes(field, table_x, cos_yz, sin_yz)
    owned = lax.psum_scatter(partial_value, "slab", scatter_dimension=0, tiled=True)
    piece = gather_line(owned, "chan", lines)
    mixed = mix(piece, spec_weight)
    spectrum = lax.all_gather(mixed, "slab", axis=0)
    spectrum = spectrum.reshape(slabs, 2, chans, KEEP // slabs, modes)
    spectrum = spectrum.transpose(2, 0, 3, 1, 4).reshape(chans * KEEP, 2 * modes)
    scale = 1.0 / (xcells * ycells * zdepth * slabs)
    cos_zy, sin_zy = joined("lz,ky->klzy", (KEEP, KEEP, zdepth * ycells))
    weight = (fold * scale)[None, :, None]
    cos_zy = (cos_zy * weight).reshape(modes, -1)
    sin_zy = (sin_zy * weight).reshape(modes, -1)
    back_table = jnp.concatenate(
        [jnp.concatenate([cos_zy, sin_zy], 1), jnp.concatenate([-sin_zy, cos_zy], 1)], 0
    )
    wave = jnp.dot(spectrum, back_table, precision=PRECISE)
    wave = wave.reshape(chans, KEEP, 2, zdepth, ycells).transpose(0, 3, 2, 1, 4)
    wave = wave.reshape(chans, zdepth, 2 * KEEP, ycells)
    wide_x = jnp.concatenate([cos_x, -sin_x], 0).T

    if hubs:
        high = lax.reduce_precision(wave, 8, 7)
        low_wave = (wave - high).astype(jnp.bfloat16)
        high = high.astype(jnp.bfloat16)
        waves = jnp.concatenate([high, low_wave, high], 2)
        high_x = lax.reduce_precision(wide_x, 8, 7)
        low_x = (wide_x - high_x).astype(jnp.bfloat16)
        high_x = high_x.astype(jnp.bfloat16)
        table = jnp.concatenate([high_x, high_x, low_x], 1)
        out = None
        for (mine, recv), start in zip(parts, starts):
            out = finish_chunk(table, bias_rows, waves, mine, recv, out, start, zdepth)
        return out[None]

    spread = lax.all_to_all(field, "chan", split_axis=2, concat_axis=0, tiled=True)
    mapped = jnp.einsum("oc,czxy->ozxy", local_weight, spread, preferred_element_type=jnp.float32)
    local = lax.all_to_all(mapped, "chan", split_axis=0, concat_axis=2, tiled=True)
    inverse = product("xk,ozky->ozxy", wide_x, wave)
    total = inverse + local + bias_rows[:, :, None]
    return jax.nn.gelu(total, approximate=False).astype(jnp.bfloat16)[None]


def solution(mesh):
    slabs, lines = mesh.shape["slab"], mesh.shape["chan"]
    placed = (P(None, "chan", "slab", None, None), P(), P(), P(None, "chan", None, "slab"))

    def body(field, local_weight, bias, spec_weight):
        return on_device(slabs, lines, field, local_weight, bias, spec_weight)

    return jax.shard_map(
        body,
        mesh=mesh,
        in_specs=placed,
        out_specs=P(None, "chan", "slab", None, None),
        check_vma=False,
    )
```

time: 1570 us -> 1050 us (0.67)
  blocking collectives: 608 us -> 0 us
  local copies, waits for them, and re-layouts: 537 us -> 132 us
  starting transfers between devices: 9.79 us -> 358 us
  matrix products: 314 us -> 46.4 us
  Pallas kernels: 0 us -> 223 us
  waiting for transfers between devices: 67.3 us -> 207 us
  other arithmetic: 12.9 us -> 57.1 us
    unnamed x21 -> x64, local copies, waits for them, and re-layouts: 411 us -> 14.9 us
    all_to_all x1 -> x0, blocking collectives: 369 us -> none  [on_device(): lax.all_to_all(field, 'chan', split_axis=3, concat_axis=1, tiled=True)]
    ppermute x0 -> x39, starting transfers between devices: none -> 358 us  [the longest x27 328 us: on_device(): lax.ppermute(send, 'chan', pairs)]
    dot_general x20 -> x3, matrix products: 314 us -> 46.4 us  [the longest x1 22 us: forward_modes(): four = jnp.dot(section, both, precision=PRECISE)]
    all_gather x1 -> x0, blocking collectives: 239 us -> none  [on_device(): piece = lax.all_gather(owned, 'chan', axis=2, tiled=True)]
    pallas_call x0 -> x18, Pallas kernels: none -> 223 us  [the longest x9 125 us: map_chunk(): pl.pallas_call(map_kernel, grid=(depth,), in_specs=[pl.BlockSpec(kron.sha...]
    ppermute x0 -> x39, waiting for transfers between devices: none -> 207 us  [the longest x9 134 us: on_device(): parts.append((mine, lax.ppermute(part, 'chan', back)))]
    all_to_all x3 -> x0, local copies, waits for them, and re-layouts: 72.9 us -> none  [the longest x2 45.6 us: on_device(): lax.all_to_all(field, 'chan', split_axis=3, concat_axis=1, tiled=True)]
  transfers between devices with their start and end apart: 3 -> 41, of which waited for: 2 -> 10; matrix products, arithmetic and copies ran while one was open for 36% -> 20% of each run, Pallas kernels for 0% -> 21%
where the time goes in v1:
time: 1050 us; the launch traced here: 1040 us
  starting transfers between devices  358 us (34%)
  Pallas kernels  223 us (21%)
  waiting for transfers between devices  207 us (20%)
  local copies, waits for them, and re-layouts  132 us (13%)
  other arithmetic  57.1 us (5%)
  matrix products  46.4 us (4%)
  between operations  14.6 us (1%)
    ppermute x27, starting transfers between devices, on_device(): lax.ppermute(send, 'chan', pairs)  328 us
    ppermute x9, waiting for transfers between devices, on_device(): parts.append((mine, lax.ppermute(part, 'chan', back)))  134 us
    pallas_call x9, Pallas kernels, map_chunk(): pl.pallas_call(map_kernel, grid=(depth,), in_specs=[pl.BlockSpec(kron.sha...  125 us
    pallas_call x9, Pallas kernels, finish_chunk(): pl.pallas_call(finish_kernel, grid=(chans // part, depth), in_specs=specs...  97.6 us
    ppermute x27, waiting for transfers between devices, on_device(): lax.ppermute(send, 'chan', pairs)  73 us
    mul x1, local copies, waits for them, and re-layouts, on_device(): pair_weight[:, None, :, None] * eye[None, :, None, :]  57.6 us
    dot_general x1, matrix products, forward_modes(): four = jnp.dot(section, both, precision=PRECISE)  22 us
  transfers between devices with their start and end apart: 41, of which 10 were waited for; matrix products, arithmetic and copies ran while one was open for 20% of the time, Pallas kernels for 21%

profile of v1, /device:TPU:0, one launch (start us, length us, event | category | flops | bytes accessed | tf_op | source)
XLA Modules:
  0.0 1038.7 jit_solution(865229743491828738)
XLA Ops:
  41.4 11.0 %copy.51 = f32[32,32,16,128]{3,2,1,0:T(8,128)} copy(f32[32,32,16,128]{3,1,2,0:T(8,128)S(1)} %convolution_bitcast_fusion.1) | data formatting | bytes 16777216 | tf_op jit(solution)/shard_map/kx,czxy->ckzy/transpose | solution.py:137
  66.3 52.9 %collective-permute-start.21 = (bf16[32,2,128,128]{3,2,1,0:T(8,128)(2,1)}, bf16[32,2,128,128]{3,2,1,0:T(8,128)(2,1)}, u32[]{:S(2)}, u32[]{:S(2)}) collective-permute-start(bf16[32,2,128,128]{3,2,1,0:T(8,128)(2,1)} %get-tuple-element.105), channel_id=1, source_target_pairs={{0,1},{3,2},{4,5},{7,6},{8,9},{11,10},{12,13},{15,14},{16,17},{19,... | collective-permute-start | bytes 6291464 | tf_op jit(solution)/shard_map/ppermute | solution.py:227
  121.3 22.0 %fusion.5 = f32[32,32,2,256]{3,1,2,0:T(8,128)S(1)} fusion(f32[2,256,2048,1]{2,1,0,3:T(8,128)S(1)} %bitcast.148, f32[32,32,2048,1]{2,1,0,3:T(8,128)S(1)} %bitcast.145), kind=kOutput, calls=%fused_computation.14 | convolution fusion | flops 12884901888 | bytes 14680064 | tf_op jit(solution)/shard_map/dot_general | solution.py:140
  150.2 59.0 %collective-permute-start.8 = (bf16[32,2,128,128]{3,2,1,0:T(8,128)(2,1)}, bf16[32,2,128,128]{3,2,1,0:T(8,128)(2,1)}, u32[]{:S(2)}, u32[]{:S(2)}) collective-permute-start(bf16[32,2,128,128]{3,2,1,0:T(8,128)(2,1)} %get-tuple-element.51), channel_id=1, source_target_pairs={{0,1},{3,2},{4,5},{7,6},{8,9},{11,10},{12,13},{15,14},{16,17},{19,... | collective-permute-start | bytes 6291464 | tf_op jit(solution)/shard_map/ppermute | solution.py:227
  211.2 11.0 %broadcast_multiply_fusion = bf16[64,16,128,16]{3,2,1,0:T(8,128)(2,1)} fusion(bf16[16,16]{1,0:T(8,128)(2,1)S(1)} %fusion.27, bf16[64,128]{1,0:T(8,128)(2,1)S(1)} %maximum_maximum_fusion), kind=kLoop, calls=%fused_computation | loop fusion | flops 2097152 | bytes 4211200 | tf_op jit(solution)/shard_map/mul | solution.py:212
  222.2 57.6 %mul.162.kron_ref = bf16[1024,2048]{1,0:T(8,128)(2,1)} reshape(bf16[64,16,128,16]{3,2,1,0:T(8,128)(2,1)} %broadcast_multiply_fusion) | data formatting | bytes 8388608 | tf_op jit(solution)/shard_map/mul | solution.py:212
  281.6 15.1 %collective-permute-start.1 = (f32[2,2,32,256]{3,2,1,0:T(8,128)}, f32[2,2,32,256]{3,2,1,0:T(8,128)S(1)}, u32[]{:S(2)}, u32[]{:S(2)}) collective-permute-start(f32[2,2,32,256]{3,2,1,0:T(8,128)} %reduce-scatter.2.cloned.1.call-done), channel_id=1, source_target_pairs={{0,2},{1,3},{2,0},{3,1},{4,6},{5,7},{6,4},{7,5},{8,10},{9,11},{10,... | collective-permute-start | bytes 393224 | tf_op jit(solution)/shard_map/ppermute | solution.py:152
  298.3 15.4 %map_chunk.17 = (f32[32,2,128,128]{3,2,1,0:T(8,128)}, f32[32,2,128,128]{3,2,1,0:T(8,128)}) custom-call(bf16[1024,2048]{1,0:T(8,128)(2,1)} %mul.162.kron_ref, bf16[32,16,128,128]{3,2,1,0:T(8,128)(2,1)} %bitcast.131, bf16[32,2,128,128]{3,2,1,0:T(8,128)(2,1)S(1)} %copy-done.16, bf16[32,2,128,128]{3,2,1,0:T(8,128)(2,1)} %collective-permute-done.5.b_ref, ...), custom_call_target="tpu_custom_call" | custom-call | flops 8589934592 | bytes 16777216 | tf_op jit(solution)/shard_map/map_chunk/pallas_call | solution.py:65
  317.8 78.6 %collective-permute-start.24 = (bf16[32,2,128,128]{3,2,1,0:T(8,128)(2,1)}, bf16[32,2,128,128]{3,2,1,0:T(8,128)(2,1)}, u32[]{:S(2)}, u32[]{:S(2)}) collective-permute-start(bf16[32,2,128,128]{3,2,1,0:T(8,128)(2,1)} %get-tuple-element.57), channel_id=1, source_target_pairs={{0,1},{3,2},{4,5},{7,6},{8,9},{11,10},{12,13},{15,14},{16,17},{19,... | collective-permute-start | bytes 6291464 | tf_op jit(solution)/shard_map/ppermute | solution.py:227
  399.5 15.7 %map_chunk.16 = (f32[32,2,128,128]{3,2,1,0:T(8,128)}, f32[32,2,128,128]{3,2,1,0:T(8,128)}) custom-call(bf16[1024,2048]{1,0:T(8,128)(2,1)} %mul.162.kron_ref, bf16[32,16,128,128]{3,2,1,0:T(8,128)(2,1)} %bitcast.132, bf16[32,2,128,128]{3,2,1,0:T(8,128)(2,1)} %collective-permute-done.19.a_ref, bf16[32,2,128,128]{3,2,1,0:T(8,128)(2,1)} %collective-permute-done.21.b_ref, ...), custom_call_target="tpu_custom_call" | custom-call | flops 8589934592 | bytes 16777216 | tf_op jit(solution)/shard_map/map_chunk/pallas_call | solution.py:65
  451.0 35.4 %collective-permute-done.10.c_ref = bf16[32,2,128,128]{3,2,1,0:T(8,128)(2,1)} collective-permute-done((bf16[32,2,128,128]{3,2,1,0:T(8,128)(2,1)}, bf16[32,2,128,128]{3,2,1,0:T(8,128)(2,1)}, u32[]{:S(2)}, u32[]{:S(2)}) %collective-permute-start.10) | collective-permute-done | bytes 2097184 | tf_op jit(solution)/shard_map/ppermute | solution.py:227
  496.3 31.9 %collective-permute-done.11.b_ref = bf16[32,2,128,128]{3,2,1,0:T(8,128)(2,1)S(1)} collective-permute-done((bf16[32,2,128,128]{3,2,1,0:T(8,128)(2,1)}, bf16[32,2,128,128]{3,2,1,0:T(8,128)(2,1)S(1)}, u32[]{:S(2)}, u32[]{:S(2)}) %collective-permute-start.11) | collective-permute-done | bytes 2097184 | tf_op jit(solution)/shard_map/ppermute | solution.py:227
  543.1 54.2 %collective-permute-done.37.recv_ref = f32[32,2,128,128]{3,2,1,0:T(8,128)} collective-permute-done((f32[32,2,128,128]{3,2,1,0:T(8,128)}, f32[32,2,128,128]{3,2,1,0:T(8,128)}, u32[]{:S(2)}, u32[]{:S(2)}) %collective-permute-start.37) | collective-permute-done | bytes 4194336 | tf_op jit(solution)/shard_map/ppermute | solution.py:234
  602.7 26.3 %collective-permute-start.14 = (bf16[32,2,128,128]{3,2,1,0:T(8,128)(2,1)}, bf16[32,2,128,128]{3,2,1,0:T(8,128)(2,1)}, u32[]{:S(2)}, u32[]{:S(2)}) collective-permute-start(bf16[32,2,128,128]{3,2,1,0:T(8,128)(2,1)} %get-tuple-element.53), channel_id=1, source_target_pairs={{0,1},{3,2},{4,5},{7,6},{8,9},{11,10},{12,13},{15,14},{16,17},{19,... | collective-permute-start | bytes 6291464 | tf_op jit(solution)/shard_map/ppermute | solution.py:227
  629.6 15.5 %map_chunk.15 = (f32[32,2,128,128]{3,2,1,0:T(8,128)}, f32[32,2,128,128]{3,2,1,0:T(8,128)}) custom-call(bf16[1024,2048]{1,0:T(8,128)(2,1)} %mul.162.kron_ref, bf16[32,16,128,128]{3,2,1,0:T(8,128)(2,1)} %bitcast.133, bf16[32,2,128,128]{3,2,1,0:T(8,128)(2,1)S(1)} %collective-permute-done.6.a_ref, bf16[32,2,128,128]{3,2,1,0:T(8,128)(2,1)} %collective-permute-done.8.b_ref, ...), custom_call_target="tpu_custom_call" | custom-call | flops 8589934592 | bytes 16777216 | tf_op jit(solution)/shard_map/map_chunk/pallas_call | solution.py:65
  645.1 15.8 %map_chunk.14 = (f32[32,2,128,128]{3,2,1,0:T(8,128)}, f32[32,2,128,128]{3,2,1,0:T(8,128)}) custom-call(bf16[1024,2048]{1,0:T(8,128)(2,1)} %mul.162.kron_ref, bf16[32,16,128,128]{3,2,1,0:T(8,128)(2,1)} %bitcast.134, bf16[32,2,128,128]{3,2,1,0:T(8,128)(2,1)} %collective-permute-done.22.a_ref, bf16[32,2,128,128]{3,2,1,0:T(8,128)(2,1)} %collective-permute-done.24.b_ref, ...), custom_call_target="tpu_custom_call" | custom-call | flops 8589934592 | bytes 16777216 | tf_op jit(solution)/shard_map/map_chunk/pallas_call | solution.py:65
  672.0 44.1 %collective-permute-start.29 = (bf16[32,1,128,128]{3,2,1,0:T(8,128)(2,1)}, bf16[32,1,128,128]{3,2,1,0:T(8,128)(2,1)S(1)}, u32[]{:S(2)}, u32[]{:S(2)}) collective-permute-start(bf16[32,1,128,128]{3,2,1,0:T(8,128)(2,1)} %get-tuple-element.59), channel_id=1, source_target_pairs={{0,1},{3,2},{4,5},{7,6},{8,9},{11,10},{12,13},{15,14},{16,17},{19,... | collective-permute-start | bytes 3145736 | tf_op jit(solution)/shard_map/ppermute | solution.py:227
  719.1 17.5 %convolution_bitcast_fusion = f32[32,16,2,16,128]{4,3,1,2,0:T(8,128)} fusion(f32[2,16,128,512,1]{3,2,1,0,4:T(8,128)} %bitcast.143, f32[32,16,512,1,1]{2,1,0,3,4:T(8,128)S(1)} %reshape.126), kind=kOutput, calls=%fused_computation.17 | convolution fusion | flops 12884901888 | bytes 17825792 | tf_op jit(solution)/shard_map/dot_general | solution.py:252
  744.6 15.0 %map_chunk.13 = (f32[32,2,128,128]{3,2,1,0:T(8,128)}, bf16[32,2,128,128]{3,2,1,0:T(8,128)(2,1)}) custom-call(bf16[1024,2048]{1,0:T(8,128)(2,1)} %mul.162.kron_ref, bf16[32,16,128,128]{3,2,1,0:T(8,128)(2,1)} %bitcast.136, bf16[32,2,128,128]{3,2,1,0:T(8,128)(2,1)S(1)} %copy-done.22, bf16[32,2,128,128]{3,2,1,0:T(8,128)(2,1)S(1)} %copy-done.20, ...), custom_call_target="tpu_custom_call" | custom-call | flops 8589934592 | bytes 16777216 | tf_op jit(solution)/shard_map/map_chunk/pallas_call | solution.py:65
  766.8 15.3 %map_chunk.12 = (f32[32,2,128,128]{3,2,1,0:T(8,128)}, bf16[32,2,128,128]{3,2,1,0:T(8,128)(2,1)}) custom-call(bf16[1024,2048]{1,0:T(8,128)(2,1)} %mul.162.kron_ref, bf16[32,16,128,128]{3,2,1,0:T(8,128)(2,1)} %bitcast.137, bf16[32,2,128,128]{3,2,1,0:T(8,128)(2,1)S(1)} %copy-done.18, bf16[32,2,128,128]{3,2,1,0:T(8,128)(2,1)} %collective-permute-done.27.b_ref, ...), custom_call_target="tpu_custom_call" | custom-call | flops 8589934592 | bytes 16777216 | tf_op jit(solution)/shard_map/map_chunk/pallas_call | solution.py:65
  782.1 15.2 %map_chunk.11 = (f32[32,2,128,128]{3,2,1,0:T(8,128)}, bf16[32,2,128,128]{3,2,1,0:T(8,128)(2,1)S(1)}) custom-call(bf16[1024,2048]{1,0:T(8,128)(2,1)} %mul.162.kron_ref, bf16[32,16,128,128]{3,2,1,0:T(8,128)(2,1)} %bitcast.138, bf16[32,2,128,128]{3,2,1,0:T(8,128)(2,1)} %collective-permute-done.12.a_ref, ...), custom_call_target="tpu_custom_call" | custom-call | flops 8589934592 | bytes 16777216 | tf_op jit(solution)/shard_map/map_chunk/pallas_call | solution.py:65
  828.9 17.7 %collective-permute-done.35.recv_ref = f32[32,2,128,128]{3,2,1,0:T(8,128)} collective-permute-done((f32[32,2,128,128]{3,2,1,0:T(8,128)}, f32[32,2,128,128]{3,2,1,0:T(8,128)}, u32[]{:S(2)}, u32[]{:S(2)}) %collective-permute-start.35) | collective-permute-done | bytes 4194336 | tf_op jit(solution)/shard_map/ppermute | solution.py:234
  857.2 11.0 %pad_maximum_fusion.wave_ref = bf16[32,16,96,128]{3,2,1,0:T(8,128)(2,1)} fusion(bf16[32,16,32,128]{3,2,1,0:T(8,128)(2,1)} %get-tuple-element.115, bf16[32,16,32,128]{3,2,1,0:T(8,128)(2,1)} %get-tuple-element.114), kind=kLoop, calls=%fused_computation.1 | loop fusion | flops 37748736 | bytes 20971520 | tf_op jit(solution)/shard_map/concatenate | solution.py:261
  868.2 12.2 %finish_chunk.9.rest_0_ = bf16[32,16,128,128]{3,2,1,0:T(8,128)(2,1)} custom-call(bf16[128,96]{1,0:T(8,128)(2,1)S(1)} %pad_maximum_fusion.3.table_ref, f32[32,1,128]{2,1,0:T(1,128)S(1)} %broadcast_in_dim.43.bias_ref, bf16[32,16,96,128]{3,2,1,0:T(8,128)(2,1)} %pad_maximum_fusion.wave_ref, f32[32,2,128,128]{3,2,1,0:T(8,128)S(1)} %copy-done, ...), custom_call_target="tpu_custom_call" | custom-call | flops 62914560 | bytes 12582912 | tf_op jit(solution)/shard_map/finish_chunk/pallas_call | solution.py:120
  880.4 12.2 %finish_chunk.10.rest_0_ = bf16[32,16,128,128]{3,2,1,0:T(8,128)(2,1)} custom-call(bf16[128,96]{1,0:T(8,128)(2,1)S(1)} %pad_maximum_fusion.3.table_ref, f32[32,1,128]{2,1,0:T(1,128)S(1)} %broadcast_in_dim.43.bias_ref, bf16[32,16,96,128]{3,2,1,0:T(8,128)(2,1)} %pad_maximum_fusion.wave_ref, ...), custom_call_target="tpu_custom_call", output_to_operand_aliasing={{}: (5, {})} | custom-call | flops 62914560 | bytes 12582912 | tf_op jit(solution)/shard_map/finish_chunk/pallas_call | solution.py:120
  892.6 12.2 %finish_chunk.11.rest_0_ = bf16[32,16,128,128]{3,2,1,0:T(8,128)(2,1)} custom-call(bf16[128,96]{1,0:T(8,128)(2,1)S(1)} %pad_maximum_fusion.3.table_ref, f32[32,1,128]{2,1,0:T(1,128)S(1)} %broadcast_in_dim.43.bias_ref, bf16[32,16,96,128]{3,2,1,0:T(8,128)(2,1)} %pad_maximum_fusion.wave_ref, ...), custom_call_target="tpu_custom_call", output_to_operand_aliasing={{}: (5, {})} | custom-call | flops 62914560 | bytes 12582912 | tf_op jit(solution)/shard_map/finish_chunk/pallas_call | solution.py:120
  904.8 12.2 %finish_chunk.12.rest_0_ = bf16[32,16,128,128]{3,2,1,0:T(8,128)(2,1)} custom-call(bf16[128,96]{1,0:T(8,128)(2,1)S(1)} %pad_maximum_fusion.3.table_ref, f32[32,1,128]{2,1,0:T(1,128)S(1)} %broadcast_in_dim.43.bias_ref, bf16[32,16,96,128]{3,2,1,0:T(8,128)(2,1)} %pad_maximum_fusion.wave_ref, ...), custom_call_target="tpu_custom_call", output_to_operand_aliasing={{}: (5, {})} | custom-call | flops 62914560 | bytes 12582912 | tf_op jit(solution)/shard_map/finish_chunk/pallas_call | solution.py:120
  920.0 11.9 %finish_chunk.13.rest_0_ = bf16[32,16,128,128]{3,2,1,0:T(8,128)(2,1)} custom-call(bf16[128,96]{1,0:T(8,128)(2,1)S(1)} %pad_maximum_fusion.3.table_ref, f32[32,1,128]{2,1,0:T(1,128)S(1)} %broadcast_in_dim.43.bias_ref, bf16[32,16,96,128]{3,2,1,0:T(8,128)(2,1)} %pad_maximum_fusion.wave_ref, ...), custom_call_target="tpu_custom_call", output_to_operand_aliasing={{}: (5, {})} | custom-call | flops 62914560 | bytes 12582912 | tf_op jit(solution)/shard_map/finish_chunk/pallas_call | solution.py:120
  936.3 11.9 %finish_chunk.14.rest_0_ = bf16[32,16,128,128]{3,2,1,0:T(8,128)(2,1)} custom-call(bf16[128,96]{1,0:T(8,128)(2,1)S(1)} %pad_maximum_fusion.3.table_ref, f32[32,1,128]{2,1,0:T(1,128)S(1)} %broadcast_in_dim.43.bias_ref, bf16[32,16,96,128]{3,2,1,0:T(8,128)(2,1)} %pad_maximum_fusion.wave_ref, ...), custom_call_target="tpu_custom_call", output_to_operand_aliasing={{}: (5, {})} | custom-call | flops 62914560 | bytes 12582912 | tf_op jit(solution)/shard_map/finish_chunk/pallas_call | solution.py:120
  948.2 33.0 %collective-permute-done.32.recv_ref = bf16[32,2,128,128]{3,2,1,0:T(8,128)(2,1)S(1)} collective-permute-done((bf16[32,2,128,128]{3,2,1,0:T(8,128)(2,1)}, bf16[32,2,128,128]{3,2,1,0:T(8,128)(2,1)S(1)}, u32[]{:S(2)}, u32[]{:S(2)}) %collective-permute-start.32) | collective-permute-done | bytes 2097184 | tf_op jit(solution)/shard_map/ppermute | solution.py:234
  981.2 11.7 %finish_chunk.15.rest_0_ = bf16[32,16,128,128]{3,2,1,0:T(8,128)(2,1)} custom-call(bf16[128,96]{1,0:T(8,128)(2,1)S(1)} %pad_maximum_fusion.3.table_ref, f32[32,1,128]{2,1,0:T(1,128)S(1)} %broadcast_in_dim.43.bias_ref, bf16[32,16,96,128]{3,2,1,0:T(8,128)(2,1)} %pad_maximum_fusion.wave_ref, ...), custom_call_target="tpu_custom_call", output_to_operand_aliasing={{}: (5, {})} | custom-call | flops 62914560 | bytes 12582912 | tf_op jit(solution)/shard_map/finish_chunk/pallas_call | solution.py:120
  1010.6 14.2 %collective-permute-done.18.recv_ref = bf16[32,1,128,128]{3,2,1,0:T(8,128)(2,1)S(1)} collective-permute-done((bf16[32,1,128,128]{3,2,1,0:T(8,128)(2,1)}, bf16[32,1,128,128]{3,2,1,0:T(8,128)(2,1)S(1)}, u32[]{:S(2)}, u32[]{:S(2)}) %collective-permute-start.18) | collective-permute-done | bytes 1048608 | tf_op jit(solution)/shard_map/ppermute | solution.py:234
  (187 shorter events, 239.6 us)
Async XLA Ops:
  6.5 273.3 %reduce-scatter.2.cloned.1.call-start = ((), (), s32[]{:S(2)}) async-start(), calls=%async_computation.1 | async-start | bytes 1179648 | tf_op jit(solution)/shard_map/reduce_scatter | solution.py:238
  18.1 127.4 %collective-permute-start.4 = (bf16[32,2,128,128]{3,2,1,0:T(8,128)(2,1)}, bf16[32,2,128,128]{3,2,1,0:T(8,128)(2,1)}, u32[]{:S(2)}, u32[]{:S(2)}) collective-permute-start(bf16[32,2,128,128]{3,2,1,0:T(8,128)(2,1)} %get-tuple-element.108), channel_id=1, source_target_pairs={{0,2},{3,1},{4,6},{7,5},{8,10},{11,9},{12,14},{15,13},{16,18},{19,... | collective-permute-start | bytes 6291464 | tf_op jit(solution)/shard_map/ppermute | solution.py:227
  27.0 118.5 %collective-permute-start.5 = (bf16[32,2,128,128]{3,2,1,0:T(8,128)(2,1)}, bf16[32,2,128,128]{3,2,1,0:T(8,128)(2,1)}, u32[]{:S(2)}, u32[]{:S(2)}) collective-permute-start(bf16[32,2,128,128]{3,2,1,0:T(8,128)(2,1)} %get-tuple-element.108), channel_id=1, source_target_pairs={{0,1},{3,2},{4,5},{7,6},{8,9},{11,10},{12,13},{15,14},{16,17},{19,... | collective-permute-start | bytes 6291464 | tf_op jit(solution)/shard_map/ppermute | solution.py:227
  29.6 120.5 %collective-permute-start.19 = (bf16[32,2,128,128]{3,2,1,0:T(8,128)(2,1)}, bf16[32,2,128,128]{3,2,1,0:T(8,128)(2,1)}, u32[]{:S(2)}, u32[]{:S(2)}) collective-permute-start(bf16[32,2,128,128]{3,2,1,0:T(8,128)(2,1)} %get-tuple-element.105), channel_id=1, source_target_pairs={{1,2},{2,1},{5,6},{6,5},{9,10},{10,9},{13,14},{14,13},{17,18},{18,... | collective-permute-start | bytes 6291464 | tf_op jit(solution)/shard_map/ppermute | solution.py:227
  31.6 177.6 %collective-permute-start.20 = (bf16[32,2,128,128]{3,2,1,0:T(8,128)(2,1)}, bf16[32,2,128,128]{3,2,1,0:T(8,128)(2,1)}, u32[]{:S(2)}, u32[]{:S(2)}) collective-permute-start(bf16[32,2,128,128]{3,2,1,0:T(8,128)(2,1)} %get-tuple-element.105), channel_id=1, source_target_pairs={{0,2},{3,1},{4,6},{7,5},{8,10},{11,9},{12,14},{15,13},{16,18},{19,... | collective-permute-start | bytes 6291464 | tf_op jit(solution)/shard_map/ppermute | solution.py:227
  66.3 142.9 %collective-permute-start.21 = (bf16[32,2,128,128]{3,2,1,0:T(8,128)(2,1)}, bf16[32,2,128,128]{3,2,1,0:T(8,128)(2,1)}, u32[]{:S(2)}, u32[]{:S(2)}) collective-permute-start(bf16[32,2,128,128]{3,2,1,0:T(8,128)(2,1)} %get-tuple-element.105), channel_id=1, source_target_pairs={{0,1},{3,2},{4,5},{7,6},{8,9},{11,10},{12,13},{15,14},{16,17},{19,... | collective-permute-start | bytes 6291464 | tf_op jit(solution)/shard_map/ppermute | solution.py:227
  145.2 521.5 %all-gather.3.cloned.1.call-start = ((), (), s32[]{:S(2)}) async-start(), calls=%async_computation.2 | async-start | bytes 1179648 | tf_op jit(solution)/shard_map/all_gather | solution.py:241
  145.5 136.1 %collective-permute-start.6 = (bf16[32,2,128,128]{3,2,1,0:T(8,128)(2,1)}, bf16[32,2,128,128]{3,2,1,0:T(8,128)(2,1)S(1)}, u32[]{:S(2)}, u32[]{:S(2)}) collective-permute-start(bf16[32,2,128,128]{3,2,1,0:T(8,128)(2,1)} %get-tuple-element.51), channel_id=1, source_target_pairs={{1,2},{2,1},{5,6},{6,5},{9,10},{10,9},{13,14},{14,13},{17,18},{18,... | collective-permute-start | bytes 6291464 | tf_op jit(solution)/shard_map/ppermute | solution.py:227
  146.3 167.4 %collective-permute-start.7 = (bf16[32,2,128,128]{3,2,1,0:T(8,128)(2,1)}, bf16[32,2,128,128]{3,2,1,0:T(8,128)(2,1)}, u32[]{:S(2)}, u32[]{:S(2)}) collective-permute-start(bf16[32,2,128,128]{3,2,1,0:T(8,128)(2,1)} %get-tuple-element.51), channel_id=1, source_target_pairs={{0,2},{3,1},{4,6},{7,5},{8,10},{11,9},{12,14},{15,13},{16,18},{19,... | collective-permute-start | bytes 6291464 | tf_op jit(solution)/shard_map/ppermute | solution.py:227
  150.2 164.9 %collective-permute-start.8 = (bf16[32,2,128,128]{3,2,1,0:T(8,128)(2,1)}, bf16[32,2,128,128]{3,2,1,0:T(8,128)(2,1)}, u32[]{:S(2)}, u32[]{:S(2)}) collective-permute-start(bf16[32,2,128,128]{3,2,1,0:T(8,128)(2,1)} %get-tuple-element.51), channel_id=1, source_target_pairs={{0,1},{3,2},{4,5},{7,6},{8,9},{11,10},{12,13},{15,14},{16,17},{19,... | collective-permute-start | bytes 6291464 | tf_op jit(solution)/shard_map/ppermute | solution.py:227
  209.2 207.3 %collective-permute-start.22 = (bf16[32,2,128,128]{3,2,1,0:T(8,128)(2,1)}, bf16[32,2,128,128]{3,2,1,0:T(8,128)(2,1)}, u32[]{:S(2)}, u32[]{:S(2)}) collective-permute-start(bf16[32,2,128,128]{3,2,1,0:T(8,128)(2,1)} %get-tuple-element.57), channel_id=1, source_target_pairs={{1,2},{2,1},{5,6},{6,5},{9,10},{10,9},{13,14},{14,13},{17,18},{18,... | collective-permute-start | bytes 6291464 | tf_op jit(solution)/shard_map/ppermute | solution.py:227
  281.6 114.8 %collective-permute-start.1 = (f32[2,2,32,256]{3,2,1,0:T(8,128)}, f32[2,2,32,256]{3,2,1,0:T(8,128)S(1)}, u32[]{:S(2)}, u32[]{:S(2)}) collective-permute-start(f32[2,2,32,256]{3,2,1,0:T(8,128)} %reduce-scatter.2.cloned.1.call-done), channel_id=1, source_target_pairs={{0,2},{1,3},{2,0},{3,1},{4,6},{5,7},{6,4},{7,5},{8,10},{9,11},{10,... | collective-permute-start | bytes 393224 | tf_op jit(solution)/shard_map/ppermute | solution.py:152
  313.7 101.5 %collective-permute-start.2 = (f32[2,2,32,256]{3,2,1,0:T(8,128)S(1)}, f32[2,2,32,256]{3,2,1,0:T(8,128)S(1)}, u32[]{:S(2)}, u32[]{:S(2)}) collective-permute-start(f32[2,2,32,256]{3,2,1,0:T(8,128)S(1)} %copy-done.26), channel_id=1, source_target_pairs={{0,3},{1,0},{2,1},{3,2},{4,7},{5,4},{6,5},{7,6},{8,11},{9,8},{10,9... | collective-permute-start | bytes 393224 | tf_op jit(solution)/shard_map/ppermute | solution.py:152
  315.1 126.1 %collective-permute-start.23 = (bf16[32,2,128,128]{3,2,1,0:T(8,128)(2,1)}, bf16[32,2,128,128]{3,2,1,0:T(8,128)(2,1)}, u32[]{:S(2)}, u32[]{:S(2)}) collective-permute-start(bf16[32,2,128,128]{3,2,1,0:T(8,128)(2,1)} %get-tuple-element.57), channel_id=1, source_target_pairs={{0,2},{3,1},{4,6},{7,5},{8,10},{11,9},{12,14},{15,13},{16,18},{19,... | collective-permute-start | bytes 6291464 | tf_op jit(solution)/shard_map/ppermute | solution.py:227
  317.8 132.1 %collective-permute-start.24 = (bf16[32,2,128,128]{3,2,1,0:T(8,128)(2,1)}, bf16[32,2,128,128]{3,2,1,0:T(8,128)(2,1)}, u32[]{:S(2)}, u32[]{:S(2)}) collective-permute-start(bf16[32,2,128,128]{3,2,1,0:T(8,128)(2,1)} %get-tuple-element.57), channel_id=1, source_target_pairs={{0,1},{3,2},{4,5},{7,6},{8,9},{11,10},{12,13},{15,14},{16,17},{19,... | collective-permute-start | bytes 6291464 | tf_op jit(solution)/shard_map/ppermute | solution.py:227
  396.4 90.1 %collective-permute-start.10 = (bf16[32,2,128,128]{3,2,1,0:T(8,128)(2,1)}, bf16[32,2,128,128]{3,2,1,0:T(8,128)(2,1)}, u32[]{:S(2)}, u32[]{:S(2)}) collective-permute-start(bf16[32,2,128,128]{3,2,1,0:T(8,128)(2,1)} %get-tuple-element.52), channel_id=1, source_target_pairs={{0,2},{3,1},{4,6},{7,5},{8,10},{11,9},{12,14},{15,13},{16,18},{19,... | collective-permute-start | bytes 6291464 | tf_op jit(solution)/shard_map/ppermute | solution.py:227
  415.2 125.9 %collective-permute-start.38 = (f32[32,2,128,128]{3,2,1,0:T(8,128)}, f32[32,2,128,128]{3,2,1,0:T(8,128)}, u32[]{:S(2)}, u32[]{:S(2)}) collective-permute-start(f32[32,2,128,128]{3,2,1,0:T(8,128)} %get-tuple-element.96), channel_id=1, source_target_pairs={{1,0},{2,3},{5,4},{6,7},{9,8},{10,11},{13,12},{14,15},{17,16},{18,... | collective-permute-start | bytes 12582920 | tf_op jit(solution)/shard_map/ppermute | solution.py:234
  416.5 180.8 %collective-permute-start.37 = (f32[32,2,128,128]{3,2,1,0:T(8,128)}, f32[32,2,128,128]{3,2,1,0:T(8,128)}, u32[]{:S(2)}, u32[]{:S(2)}) collective-permute-start(f32[32,2,128,128]{3,2,1,0:T(8,128)} %get-tuple-element.91), channel_id=1, source_target_pairs={{1,0},{2,3},{5,4},{6,7},{9,8},{10,11},{13,12},{14,15},{17,16},{18,... | collective-permute-start | bytes 12582920 | tf_op jit(solution)/shard_map/ppermute | solution.py:234
  486.5 114.9 %collective-permute-start.25 = (bf16[32,2,128,128]{3,2,1,0:T(8,128)(2,1)}, bf16[32,2,128,128]{3,2,1,0:T(8,128)(2,1)S(1)}, u32[]{:S(2)}, u32[]{:S(2)}) collective-permute-start(bf16[32,2,128,128]{3,2,1,0:T(8,128)(2,1)} %get-tuple-element.58), channel_id=1, source_target_pairs={{1,2},{2,1},{5,6},{6,5},{9,10},{10,9},{13,14},{14,13},{17,18},{18,... | collective-permute-start | bytes 6291464 | tf_op jit(solution)/shard_map/ppermute | solution.py:227
  529.6 131.3 %collective-permute-start.26 = (bf16[32,2,128,128]{3,2,1,0:T(8,128)(2,1)}, bf16[32,2,128,128]{3,2,1,0:T(8,128)(2,1)}, u32[]{:S(2)}, u32[]{:S(2)}) collective-permute-start(bf16[32,2,128,128]{3,2,1,0:T(8,128)(2,1)} %get-tuple-element.58), channel_id=1, source_target_pairs={{0,2},{3,1},{4,6},{7,5},{8,10},{11,9},{12,14},{15,13},{16,18},{19,... | collective-permute-start | bytes 6291464 | tf_op jit(solution)/shard_map/ppermute | solution.py:227
  538.5 123.8 %collective-permute-start.27 = (bf16[32,2,128,128]{3,2,1,0:T(8,128)(2,1)}, bf16[32,2,128,128]{3,2,1,0:T(8,128)(2,1)}, u32[]{:S(2)}, u32[]{:S(2)}) collective-permute-start(bf16[32,2,128,128]{3,2,1,0:T(8,128)(2,1)} %get-tuple-element.58), channel_id=1, source_target_pairs={{0,1},{3,2},{4,5},{7,6},{8,9},{11,10},{12,13},{15,14},{16,17},{19,... | collective-permute-start | bytes 6291464 | tf_op jit(solution)/shard_map/ppermute | solution.py:227
  541.1 129.2 %collective-permute-start.12 = (bf16[32,2,128,128]{3,2,1,0:T(8,128)(2,1)}, bf16[32,2,128,128]{3,2,1,0:T(8,128)(2,1)}, u32[]{:S(2)}, u32[]{:S(2)}) collective-permute-start(bf16[32,2,128,128]{3,2,1,0:T(8,128)(2,1)} %get-tuple-element.53), channel_id=1, source_target_pairs={{1,2},{2,1},{5,6},{6,5},{9,10},{10,9},{13,14},{14,13},{17,18},{18,... | collective-permute-start | bytes 6291464 | tf_op jit(solution)/shard_map/ppermute | solution.py:227
  602.7 113.4 %collective-permute-start.14 = (bf16[32,2,128,128]{3,2,1,0:T(8,128)(2,1)}, bf16[32,2,128,128]{3,2,1,0:T(8,128)(2,1)}, u32[]{:S(2)}, u32[]{:S(2)}) collective-permute-start(bf16[32,2,128,128]{3,2,1,0:T(8,128)(2,1)} %get-tuple-element.53), channel_id=1, source_target_pairs={{0,1},{3,2},{4,5},{7,6},{8,9},{11,10},{12,13},{15,14},{16,17},{19,... | collective-permute-start | bytes 6291464 | tf_op jit(solution)/shard_map/ppermute | solution.py:227
  660.9 166.6 %collective-permute-start.36 = (f32[32,2,128,128]{3,2,1,0:T(8,128)}, f32[32,2,128,128]{3,2,1,0:T(8,128)}, u32[]{:S(2)}, u32[]{:S(2)}) collective-permute-start(f32[32,2,128,128]{3,2,1,0:T(8,128)} %get-tuple-element.86), channel_id=1, source_target_pairs={{1,0},{2,3},{5,4},{6,7},{9,8},{10,11},{13,12},{14,15},{17,16},{18,... | collective-permute-start | bytes 12582920 | tf_op jit(solution)/shard_map/ppermute | solution.py:234
  662.2 184.3 %collective-permute-start.35 = (f32[32,2,128,128]{3,2,1,0:T(8,128)}, f32[32,2,128,128]{3,2,1,0:T(8,128)}, u32[]{:S(2)}, u32[]{:S(2)}) collective-permute-start(f32[32,2,128,128]{3,2,1,0:T(8,128)} %get-tuple-element.81), channel_id=1, source_target_pairs={{1,0},{2,3},{5,4},{6,7},{9,8},{10,11},{13,12},{14,15},{17,16},{18,... | collective-permute-start | bytes 12582920 | tf_op jit(solution)/shard_map/ppermute | solution.py:234
  670.3 89.3 %collective-permute-start.28 = (bf16[32,1,128,128]{3,2,1,0:T(8,128)(2,1)}, bf16[32,1,128,128]{3,2,1,0:T(8,128)(2,1)S(1)}, u32[]{:S(2)}, u32[]{:S(2)}) collective-permute-start(bf16[32,1,128,128]{3,2,1,0:T(8,128)(2,1)} %get-tuple-element.59), channel_id=1, source_target_pairs={{1,2},{2,1},{5,6},{6,5},{9,10},{10,9},{13,14},{14,13},{17,18},{18,... | collective-permute-start | bytes 3145736 | tf_op jit(solution)/shard_map/ppermute | solution.py:227
  672.0 88.4 %collective-permute-start.29 = (bf16[32,1,128,128]{3,2,1,0:T(8,128)(2,1)}, bf16[32,1,128,128]{3,2,1,0:T(8,128)(2,1)S(1)}, u32[]{:S(2)}, u32[]{:S(2)}) collective-permute-start(bf16[32,1,128,128]{3,2,1,0:T(8,128)(2,1)} %get-tuple-element.59), channel_id=1, source_target_pairs={{0,1},{3,2},{4,5},{7,6},{8,9},{11,10},{12,13},{15,14},{16,17},{19,... | collective-permute-start | bytes 3145736 | tf_op jit(solution)/shard_map/ppermute | solution.py:227
  799.6 117.3 %collective-permute-start.34 = (bf16[32,2,128,128]{3,2,1,0:T(8,128)(2,1)}, bf16[32,2,128,128]{3,2,1,0:T(8,128)(2,1)S(1)}, u32[]{:S(2)}, u32[]{:S(2)}) collective-permute-start(bf16[32,2,128,128]{3,2,1,0:T(8,128)(2,1)} %get-tuple-element.76), channel_id=1, source_target_pairs={{1,0},{2,3},{5,4},{6,7},{9,8},{10,11},{13,12},{14,15},{17,16},{18,... | collective-permute-start | bytes 6291464 | tf_op jit(solution)/shard_map/ppermute | solution.py:234
  801.9 134.4 %collective-permute-start.33 = (bf16[32,2,128,128]{3,2,1,0:T(8,128)(2,1)}, bf16[32,2,128,128]{3,2,1,0:T(8,128)(2,1)S(1)}, u32[]{:S(2)}, u32[]{:S(2)}) collective-permute-start(bf16[32,2,128,128]{3,2,1,0:T(8,128)(2,1)} %get-tuple-element.71), channel_id=1, source_target_pairs={{1,0},{2,3},{5,4},{6,7},{9,8},{10,11},{13,12},{14,15},{17,16},{18,... | collective-permute-start | bytes 6291464 | tf_op jit(solution)/shard_map/ppermute | solution.py:234
  808.9 172.4 %collective-permute-start.32 = (bf16[32,2,128,128]{3,2,1,0:T(8,128)(2,1)}, bf16[32,2,128,128]{3,2,1,0:T(8,128)(2,1)S(1)}, u32[]{:S(2)}, u32[]{:S(2)}) collective-permute-start(bf16[32,2,128,128]{3,2,1,0:T(8,128)(2,1)} %copy-done.23), channel_id=1, source_target_pairs={{1,0},{2,3},{5,4},{6,7},{9,8},{10,11},{13,12},{14,15},{17,16},{18,... | collective-permute-start | bytes 6291464 | tf_op jit(solution)/shard_map/ppermute | solution.py:234
  827.6 176.2 %collective-permute-start.31 = (bf16[32,1,128,128]{3,2,1,0:T(8,128)(2,1)}, bf16[32,1,128,128]{3,2,1,0:T(8,128)(2,1)}, u32[]{:S(2)}, u32[]{:S(2)}) collective-permute-start(bf16[32,1,128,128]{3,2,1,0:T(8,128)(2,1)} %get-tuple-element.61), channel_id=1, source_target_pairs={{1,0},{2,3},{5,4},{6,7},{9,8},{10,11},{13,12},{14,15},{17,16},{18,... | collective-permute-start | bytes 3145736 | tf_op jit(solution)/shard_map/ppermute | solution.py:234
  846.5 178.3 %collective-permute-start.18 = (bf16[32,1,128,128]{3,2,1,0:T(8,128)(2,1)}, bf16[32,1,128,128]{3,2,1,0:T(8,128)(2,1)S(1)}, u32[]{:S(2)}, u32[]{:S(2)}) collective-permute-start(bf16[32,1,128,128]{3,2,1,0:T(8,128)(2,1)} %get-tuple-element.56), channel_id=1, source_target_pairs={{1,0},{2,3},{5,4},{6,7},{9,8},{10,11},{13,12},{14,15},{17,16},{18,... | collective-permute-start | bytes 3145736 | tf_op jit(solution)/shard_map/ppermute | solution.py:234
  (40 other events, 865.5 us)
Sparse Core Ops, SparseCore 0:
  145.3 36.1 reduce-scatter.1
  629.8 21.6 all-gather.2
